TPU v7x, 32 devices: a whole 2x2x4 slice. The times are simulated.
32 devices in a mesh: dp: 8 (over z, core), mp: 4 (over y, x).
Axes of the slice: x: 2, y: 2, z: 4, core: 2. Of those that a mesh axis runs over, the one named last changes fastest.
Arguments:
- hidden_in: bfloat16 [16, 512, 8192], P('dp', None, 'mp'), may hold values from -6 to 6
- query_act: bfloat16 [16, 512, 8192], P('dp', None, 'mp'), may hold values from -6 to 6
- key_act: bfloat16 [16, 512, 1024], P('dp'), may hold values from -6 to 6
- value_act: bfloat16 [16, 512, 1024], P('dp'), may hold values from -6 to 6
- ctx_grad: bfloat16 [16, 512, 8192], P('dp', None, 'mp'), may hold values from -6 to 6
- segment_ids: int32 [16, 512], P('dp'), may hold values from 0 to 3, never falling along the last dimension, each value on 1 to 256 neighbouring positions
- down_query: bfloat16 [8192, 128], P('mp'), may hold values from -0.0625 to 0.0625
- up_query: bfloat16 [128, 8192], P(None, 'mp'), may hold values from -0.5 to 0.5
- down_value: bfloat16 [8192, 128], P('mp'), may hold values from -0.0625 to 0.0625
- up_value: bfloat16 [128, 1024], replicated, may hold values from -0.5 to 0.5
- block_rows: int32 [3, 8192], P(None, 'mp'), may hold values from 0 to 63
- tile_rows: int32 [3, 8192], P(None, 'mp'), may hold values from 0 to 7
- block_value: int32 [1024], replicated, may hold values from 0 to 63
- tile_value: int32 [1024], replicated, may hold values from 0 to 7
- tile_bank: bfloat16 [8, 128, 128], replicated, may hold values from -0.5 to 0.5
- seed_feats: bfloat16 [256, 8192], P('dp', 'mp'), may hold values from -6 to 6
Outputs:
- scores: float32 [16, 256], P('dp', 'mp')
All inputs are finite; a program needn't handle non-finite values.
Results may differ from a plain program's by a relative error of at most 0.022.
Values may be sent and summed in bfloat16 or wider, within the bound.
A program may use at most 192 MiB of HBM per device.

v0:
```python
import functools
import math

import jax
import jax.numpy as jnp
from jax import lax
from jax.experimental import pallas as pl
from jax.experimental.pallas import tpu as pltpu
from jax.sharding import PartitionSpec as P

H = 64
KVH = 8
DH = 128
R = 128
K = 8192
PB = 128
NT = 8
KB = K // PB
REACH = 256

EPS = 1e-06
BF = jnp.bfloat16
F32 = jnp.float32
NEG = -1e30


def dot(a, b):
    return jnp.dot(a, b, preferred_element_type=F32)


def dot_nt(a, b):
    return lax.dot_general(a, b, (((1,), (1,)), ((), ())), preferred_element_type=F32)


def build_mask(seg_ref, mask_ref, b):
    seq = mask_ref.shape[0]
    row = seg_ref[b : b + 1, :].astype(F32)
    column = jnp.broadcast_to(row, (128, seq)).T[:, :1]
    for lo in range(0, seq, REACH):
        shape = (seq, REACH)
        key_pos = lax.broadcasted_iota(jnp.int32, shape, 0)
        query_pos = lax.broadcasted_iota(jnp.int32, shape, 1) + lo
        same = column == row[:, lo : lo + REACH]
        allowed = jnp.logical_and(key_pos <= query_pos, same)
        mask_ref[:, lo : lo + REACH] = jnp.where(allowed, 0.0, NEG)


def attend(b, g, repeats, q_v, c_v, k_v, v_v, mask, vsum, dq_t, vg):
    seq = mask.shape[0]
    kv_cols = slice(g * DH, (g + 1) * DH)
    keys = k_v[b, :, kv_cols]
    vals = v_v[b, :, kv_cols]
    keys_t = keys.T
    scale = 1.0 / math.sqrt(DH)
    vsum[...] = jnp.zeros_like(vsum)

    def head(h, carry):
        cols = pl.ds(pl.multiple_of((g * repeats + h) * DH, DH), DH)
        for lo in range(0, seq, REACH):
            first = max(lo - REACH, 0)
            rows = slice(first, lo + REACH)
            quer = q_v[b, lo : lo + REACH, cols]
            cot = c_v[b, lo : lo + REACH, cols]
            logit = dot_nt(keys[rows], quer) + mask[rows, lo : lo + REACH]
            prob_grad = dot_nt(vals[rows], cot)
            top = jnp.max(logit, axis=0, keepdims=True)
            terms = jnp.exp2((logit - top) * (scale * math.log2(math.e)))
            inv = 1.0 / jnp.sum(terms, axis=0, keepdims=True)
            probs = terms * inv
            delta = jnp.sum(probs * prob_grad, axis=0, keepdims=True)
            logit_grad = (probs * (prob_grad - delta)).astype(BF)
            vsum[rows, :] += dot(probs.astype(BF), cot)
            dq = dot(keys_t[:, rows], logit_grad) * scale
            dq_t[b, cols, lo : lo + REACH] = dq.astype(BF)
        return carry

    lax.fori_loop(0, repeats, head, 0)
    vg[b, :, kv_cols] = vsum[...].astype(BF)


def back_partial(b, kv_count, upq, upv, dq_t, vg):
    back_q = dot(upq[...], dq_t[b])
    back_v = jnp.zeros((R, vg.shape[1]), F32)
    for g in range(kv_count):
        cols = slice(g * DH, (g + 1) * DH)
        back_v += dot_nt(upv[:, cols], vg[b, :, cols])
    return back_q, back_v


def attention_kernel(
    kv_count, repeats,
    hid, que, key, val, ctx, seg, downq, upq_h, downv, upv_h,
    dq_t, vg, low, back,
    h_v, q_v, c_v, k_v, v_v, dn, upq, upv, mask, vsum, sems,
):
    m = lax.axis_index("mp")
    heads = kv_count * repeats
    kv_first = m * heads // (H // KVH)
    kv_cols = pl.ds(pl.multiple_of(kv_first * DH, DH), kv_count * DH)
    cands = que.shape[0]
    count = [0]

    def load(src, dst):
        copy = pltpu.make_async_copy(src, dst, sems.at[count[0]])
        count[0] += 1
        copy.start()
        return copy

    kv_copies = [load(key.at[:, :, kv_cols], k_v), load(val.at[:, :, kv_cols], v_v)]
    tok = [[load(que.at[b], q_v.at[b]), load(ctx.at[b], c_v.at[b])] for b in range(cands)]
    late = [load(hid.at[b], h_v.at[b]) for b in range(cands)]
    late += [load(downq, dn.at[:, :R]), load(downv, dn.at[:, R:]), load(upq_h, upq)]
    late += [load(upv_h.at[:, kv_cols], upv)]
    for copy in kv_copies:
        copy.wait()
    for b in range(cands):
        build_mask(seg, mask, b)
        for copy in tok[b]:
            copy.wait()
        for g in range(kv_count):
            attend(b, g, repeats, q_v, c_v, k_v, v_v, mask, vsum, dq_t, vg)
        if b == 0:
            for copy in late:
                copy.wait()
            for c in range(cands):
                low[c] = dot(h_v[c], dn[...]).astype(BF)
        back_q, back_v = back_partial(b, kv_count, upq, upv, dq_t, vg)
        back[b, :R, :] = back_q.astype(BF)
        back[b, R:, :] = back_v.astype(BF)


CHUNK = 256


def bucket_add(sums, ids, grads, transposed):
    buckets = sums.shape[0]
    spots = lax.broadcasted_iota(jnp.int32, (buckets, ids.shape[1]), 0)
    hot = jnp.where(spots == ids, 1.0, 0.0).astype(BF)
    sums[...] += (dot_nt if transposed else dot)(hot, grads)


def add_upq(sums, ids, dq_t, low):
    cands, width = dq_t.shape[0], dq_t.shape[1]
    chunk = min(CHUNK, width)

    def step(i, carry):
        rows = pl.ds(pl.multiple_of(i * chunk, chunk), chunk)
        grads = [dot(dq_t[b, rows, :], low[b, :, :R]) for b in range(cands)]
        bucket_add(sums, ids[2:3, rows], jnp.concatenate(grads, axis=1).astype(BF), False)
        return carry

    lax.fori_loop(0, width // chunk, step, 0)


def add_upv(sums, ids, vg, low):
    cands, width = vg.shape[0], vg.shape[2]
    grads = [dot(vg[b].T, low[b, :, R:]) for b in range(cands)]
    bucket_add(sums, ids[...], jnp.concatenate(grads, axis=1).astype(BF), False)


def add_down(sums, ids, h_v, back):
    cands, width = h_v.shape[0], h_v.shape[2]
    chunk = min(CHUNK, width)

    def step(i, carry):
        cols = pl.ds(pl.multiple_of(i * chunk, chunk), chunk)
        grads = [dot(back[b], h_v[b, :, cols]).astype(BF) for b in range(cands)]
        for j in range(2):
            part = jnp.concatenate([grad[j * R : (j + 1) * R] for grad in grads], axis=0)
            bucket_add(sums, ids[j : j + 1, cols], part, True)
        return carry

    lax.fori_loop(0, width // chunk, step, 0)


def project(sums, bank, b):
    total = jnp.zeros((KB, PB), F32)
    for t in range(NT):
        part = sums[t * KB : (t + 1) * KB, b * R : (b + 1) * R].astype(BF)
        total += dot(part, bank[t])
    return total


def feature_kernel(hid, dq_t, vg, low, back, ids, ids_v, bank, feats, sums):
    sums[...] = jnp.zeros_like(sums)
    add_upq(sums, ids, dq_t, low)
    add_upv(sums, ids_v, vg, low)
    add_down(sums, ids, hid, back)
    for b in range(hid.shape[0]):
        feats[b] = project(sums, bank, b).astype(BF)


ANY = pl.BlockSpec(memory_space=pl.ANY)
VMEM = pl.BlockSpec(memory_space=pltpu.VMEM)


def local(
    hidden_in, query_act, key_act, value_act, ctx_grad, segment_ids,
    down_query, up_query, down_value, up_value,
    block_rows, tile_rows, block_value, tile_value, tile_bank, seed_feats,
):
    cands, seq, width = query_act.shape
    heads = width // DH
    kv_count = max(heads // (H // KVH), 1)
    repeats = heads // kv_count
    kvw = kv_count * DH
    kv_first = lax.axis_index("mp") * heads // (H // KVH)
    seeds_all = lax.all_gather(seed_feats, "dp", axis=0, tiled=True)
    ids = tile_rows * KB + block_rows
    ids_v = lax.dynamic_slice_in_dim(tile_value * KB + block_value, kv_first * DH, kvw, 0)[None]
    dq_t, vg, low, back = pl.pallas_call(
        functools.partial(attention_kernel, kv_count, repeats),
        out_shape=(
            jax.ShapeDtypeStruct((cands, width, seq), BF),
            jax.ShapeDtypeStruct((cands, seq, kvw), BF),
            jax.ShapeDtypeStruct((cands, seq, 2 * R), BF),
            jax.ShapeDtypeStruct((cands, 2 * R, seq), BF),
        ),
        in_specs=[ANY] * 5 + [VMEM] + [ANY] * 4,
        out_specs=(VMEM,) * 4,
        scratch_shapes=[
            pltpu.VMEM((cands, seq, width), BF),
            pltpu.VMEM((cands, seq, width), BF),
            pltpu.VMEM((cands, seq, width), BF),
            pltpu.VMEM((cands, seq, kvw), BF),
            pltpu.VMEM((cands, seq, kvw), BF),
            pltpu.VMEM((width, 2 * R), BF),
            pltpu.VMEM((R, width), BF),
            pltpu.VMEM((R, kvw), BF),
            pltpu.VMEM((seq, seq), F32),
            pltpu.VMEM((seq, DH), F32),
            pltpu.SemaphoreType.DMA((6 + 3 * cands,)),
        ],
        compiler_params=pltpu.CompilerParams(vmem_limit_bytes=56 << 20),
        cost_estimate=pl.CostEstimate(
            flops=cands * heads * seq * seq * DH * 8, bytes_accessed=16 << 20,
            transcendentals=cands * heads * seq * seq,
        ),
        name="attention",
    )(hidden_in, query_act, key_act, value_act, ctx_grad, segment_ids,
      down_query, up_query, down_value, up_value)
    low, back = lax.psum((low, back), "mp")
    feats = pl.pallas_call(
        feature_kernel,
        out_shape=jax.ShapeDtypeStruct((cands, KB, PB), BF),
        in_specs=[VMEM] * 8,
        out_specs=VMEM,
        scratch_shapes=[pltpu.VMEM((KB * NT, cands * R), F32)],
        compiler_params=pltpu.CompilerParams(vmem_limit_bytes=56 << 20),
        cost_estimate=pl.CostEstimate(
            flops=cands * seq * width * R * 8, bytes_accessed=8 << 20, transcendentals=0
        ),
        name="features",
    )(hidden_in, dq_t, vg, low, back, ids, ids_v, tile_bank)
    feat_slice = lax.psum_scatter(
        feats.reshape(cands, K), "mp", scatter_dimension=1, tiled=True
    ).astype(F32)
    feat_square = jnp.sum(feat_slice * feat_slice, axis=1)
    partial_value = jnp.einsum(
        "bk,sk->bs", feat_slice.astype(BF), seeds_all, preferred_element_type=F32
    )
    total_square = lax.psum(feat_square, "mp")
    numerator = lax.psum_scatter(partial_value, "mp", scatter_dimension=1, tiled=True)
    return numerator * lax.rsqrt(total_square / K + EPS)[:, None] * K ** (-0.5)


def solution(mesh):
    return jax.shard_map(
        local,
        mesh=mesh,
        in_specs=(
            P("dp", None, "mp"),
            P("dp", None, "mp"),
            P("dp", None, None),
            P("dp", None, None),
            P("dp", None, "mp"),
            P("dp", None),
            P("mp", None),
            P(None, "mp"),
            P("mp", None),
            P(),
            P(None, "mp"),
            P(None, "mp"),
            P(),
            P(),
            P(),
            P("dp", "mp"),
        ),
        out_specs=P("dp", "mp"),
        check_vma=False,
    )
```

profile of v0, /device:TPU:0, one launch (start us, length us, event | category | flops | bytes accessed | tf_op | source)
XLA Modules:
  0.0 206.7 jit_solution(13399822974496284863)
XLA Ops:
  7.4 0.0 all-reduce.3.cloned.1.call-start
  7.4 0.0 copy-start.2
  7.4 0.0 copy-start.3
  7.4 0.0 copy-start
  7.4 0.0 copy-start.1
  7.4 45.4 %attention.1 = (bf16[2,2048,512]{2,1,0:T(8,128)(2,1)}, bf16[2,512,256]{2,1,0:T(8,128)(2,1)}, bf16[2,512,256]{2,1,0:T(8,128)(2,1)}, bf16[2,256,512]{2,1,0:T(8,128)(2,1)}) custom-call(bf16[2,512,2048]{2,1,0:T(8,128)(2,1)} %hid.3, bf16[2,512,2048]{2,1,0:T(8,128)(2,1)} %que.1, bf16[2,512,1024]{2,1,0:T(8,128)(2,1)} %key.1, bf16[2,512,1024]{2,1,0:T(8,128)(2,1)} %val.1, ...), custom_call_target="tpu_custom_call" | custom-call | flops 8589934592 | bytes 16777216 | tf_op jit(solution)/shard_map/attention/pallas_call | solution.py:211
  52.8 0.0 all-reduce.3.cloned.1.call-update
  52.8 0.0 reduce-scatter.7.cloned.1.call-start
  52.9 0.0 copy-done.2
  52.9 0.0 copy-done.3
  52.9 0.6 dynamic_slice.3
  53.5 0.0 copy-done
  53.5 0.0 copy-done.1
  53.5 0.6 multiply_add_fusion.ids
  54.2 54.2 %all-reduce.3.cloned.1.call-done = (bf16[2,512,256]{2,1,0:T(8,128)(2,1)}, bf16[2,256,512]{2,1,0:T(8,128)(2,1)}) async-done(((bf16[2,512,256]{2,1,0:T(8,128)(2,1)}, bf16[2,256,512]{2,1,0:T(8,128)(2,1)}), (bf16[2,512,256]{2,1,0:T(8,128)(2,1)}, bf16[2,256,512]{2,1,0:T(8,128)(2,1)})) %all-reduce.3.cloned.1.call-update) | async-done | bytes 1048592 | tf_op jit(solution)/shard_map/psum | solution.py:242
  108.4 15.0 %features.1 = bf16[2,64,128]{2,1,0:T(8,128)(2,1)} custom-call(bf16[2,512,2048]{2,1,0:T(8,128)(2,1)} %hid.3, bf16[2,2048,512]{2,1,0:T(8,128)(2,1)} %get-tuple-element.9.dq_t, bf16[2,512,256]{2,1,0:T(8,128)(2,1)} %get-tuple-element.10.vg, bf16[2,512,256]{2,1,0:T(8,128)(2,1)} %get-tuple-element.13.low, bf16[2,256,512]{2,1,0:T(8,128)(2,1)} %get-tuple-element.14.back, ...), custom_call_target="tpu_custom_call" | custom-call | flops 2147483648 | bytes 8388608 | tf_op jit(solution)/shard_map/features/pallas_call | solution.py:243
  123.4 2.6 %copy.21 = bf16[2,64,128]{0,2,1:T(8,128)(2,1)} copy(bf16[2,64,128]{2,1,0:T(8,128)(2,1)} %features.1) | data formatting | bytes 65536
  126.0 0.0 reduce-scatter.7.cloned.1.call-update
  126.0 0.0 all-gather.2.cloned.1.call-start
  126.0 0.5 all-gather.2.cloned.1.call-update
  126.6 0.0 reduce-scatter.9.cloned.1.call-start
  126.6 34.7 %reduce-scatter.7.cloned.1.call-done = bf16[2048,2]{1,0:T(8,128)(2,1)} async-done(((bf16[8192,2]{1,0:T(8,128)(2,1)}), bf16[2048,2]{1,0:T(8,128)(2,1)}) %reduce-scatter.7.cloned.1.call-update) | async-done | bytes 8208
  161.3 1.2 copy.18
  162.6 0.1 multiply_reduce_fusion
  162.7 8.9 %psum.23 = f32[2]{0:T(128)S(1)} all-reduce(f32[2]{0:T(128)S(1)} %multiply_reduce_fusion), channel_id=1, replica_groups=mesh['dp'=8,'mp'=4] {'mp'}, use_global_device_ids=true, to_apply=%region_5.6 | all-reduce | flops 2 | bytes 16 | tf_op jit(solution)/shard_map/psum | solution.py:262
  171.7 0.0 all-gather.2.cloned.1.call-done
  171.7 2.5 %convolution_bitcast_fusion = f32[256,2]{1,0:T(8,128)} fusion(bf16[256,2048]{1,0:T(8,128)(2,1)} %all-gather.2.cloned.1.call-done, bf16[2048,2]{1,0:T(8,128)(2,1)} %reduce-scatter.7.cloned.1.call-done), kind=kOutput, calls=%fused_computation | convolution fusion | flops 2097152 | bytes 1058816
  174.1 0.0 reduce-scatter.9.cloned.1.call-update
  174.2 23.9 %reduce-scatter.9.cloned.1.call-done = f32[64,2]{1,0:T(8,128)} async-done(((f32[256,2]{1,0:T(8,128)}), f32[64,2]{1,0:T(8,128)}) %reduce-scatter.9.cloned.1.call-update) | async-done | bytes 528
  198.1 0.8 copy.20
  198.9 0.6 multiply_multiply_fusion
  (2 shorter events, 0.0 us)
Async XLA Ops:
  7.4 101.0 %all-reduce.3.cloned.1.call-start = ((), (), s32[]{:S(2)}) async-start(), calls=%async_computation.5 | async-start | bytes 2097152 | tf_op jit(solution)/shard_map/psum | solution.py:242
  7.4 45.5 %copy-start.2 = (s32[1024]{0:T(1024)S(1)}, s32[1024]{0:T(1024)}, u32[]{:S(2)}) copy-start(s32[1024]{0:T(1024)} %param.28) | copy-start | bytes 12292
  7.4 45.5 %copy-start.3 = (s32[1024]{0:T(1024)S(1)}, s32[1024]{0:T(1024)}, u32[]{:S(2)}) copy-start(s32[1024]{0:T(1024)} %param.29) | copy-start | bytes 12292
  7.4 46.2 %copy-start = (s32[3,2048]{1,0:T(4,128)S(1)}, s32[3,2048]{1,0:T(4,128)}, u32[]{:S(2)}) copy-start(s32[3,2048]{1,0:T(4,128)} %param.26) | copy-start | bytes 73732
  7.4 46.2 %copy-start.1 = (s32[3,2048]{1,0:T(4,128)S(1)}, s32[3,2048]{1,0:T(4,128)}, u32[]{:S(2)}) copy-start(s32[3,2048]{1,0:T(4,128)} %param.27) | copy-start | bytes 73732
  52.8 108.5 %reduce-scatter.7.cloned.1.call-start = ((), (), s32[]{:S(2)}) async-start(), calls=%async_computation.3 | async-start | bytes 2621440
  126.0 45.7 %all-gather.2.cloned.1.call-start = ((), (), s32[]{:S(2)}) async-start(), calls=%async_computation.2 | async-start | bytes 1179648 | tf_op jit(solution)/shard_map/all_gather | solution.py:208
  126.6 71.5 %reduce-scatter.9.cloned.1.call-start = ((), (), s32[]{:S(2)}) async-start(), calls=%async_computation.4 | async-start | bytes 163840
Sparse Core Ops, SparseCore 0:
  52.9 55.4 all-reduce.2
  126.1 35.1 reduce-scatter.6
  174.3 23.7 reduce-scatter.8
Sparse Core Ops, SparseCore 1:
  128.1 21.9 all-gather.1
where the time goes:
time: 207 us
  waiting for transfers between devices  113 us (55%)
  Pallas kernels  60.4 us (29%)
  between operations  14.6 us (7%)
  blocking collectives  8.92 us (4%)
  local copies, waits for them, and re-layouts  5.32 us (3%)
  matrix products  2.48 us (1%)
    unnamed x6, waiting for transfers between devices  59.2 us
    psum x1, waiting for transfers between devices, local(): low, back = lax.psum((low, back), 'mp')  54.2 us
    pallas_call x1, Pallas kernels, local(): pl.pallas_call(functools.partial(attention_kernel, kv_count, repeats), ou...  45.4 us
    pallas_call x1, Pallas kernels, local(): pl.pallas_call(feature_kernel, out_shape=jax.ShapeDtypeStruct((cands, KB,...  15 us
    psum x1, blocking collectives, local(): total_square = lax.psum(feat_square, 'mp')  8.92 us
    unnamed x11, local copies, waits for them, and re-layouts  4.68 us
  transfers between devices with their start and end apart: 4, of which 3 were waited for; matrix products, arithmetic and copies ran while one was open for 1% of the time, Pallas kernels for 0%

commit v1 on v0

--- a/solution.py
+++ b/solution.py
@@ -87,17 +87,79 @@
     return back_q, back_v
 
 
-def attention_kernel(
-    kv_count, repeats,
-    hid, que, key, val, ctx, seg, downq, upq_h, downv, upv_h,
-    dq_t, vg, low, back,
-    h_v, q_v, c_v, k_v, v_v, dn, upq, upv, mask, vsum, sems,
+MESH = pl.DeviceIdType.MESH
+
+
+def meet(n):
+    barrier = pltpu.get_barrier_semaphore()
+    me = lax.axis_index("mp")
+    for k in range(1, n):
+        peer = (lax.axis_index("dp"), lax.rem(me + k, n))
+        pl.semaphore_signal(barrier, inc=1, device_id=peer, device_id_type=MESH)
+    pl.semaphore_wait(barrier, n - 1)
+
+
+def spread(n, source, target, send, recv):
+    me = lax.axis_index("mp")
+    copies = []
+    for k in range(1, n):
+        peer = lax.rem(me + k, n)
+        copy = pltpu.make_async_remote_copy(
+            src_ref=source(peer),
+            dst_ref=target(k),
+            send_sem=send.at[k - 1],
+            recv_sem=recv.at[k - 1],
+            device_id=(lax.axis_index("dp"), peer),
+            device_id_type=MESH,
+        )
+        copy.start()
+        copies.append(copy)
+    return copies
+
+
+def finish(copies):
+    for copy in copies:
+        copy.wait()
+
+
+class Reduce:
+    def __init__(self, n, part, slots, full, sems):
+        self.n, self.part, self.slots, self.full, self.sems = n, part, slots, full, sems
+
+    def scatter(self):
+        self.first = spread(
+            self.n, lambda peer: self.part.at[peer], lambda k: self.slots.at[k - 1],
+            self.sems.at[0], self.sems.at[1],
+        )
+
+    def gather(self):
+        finish(self.first)
+        me = lax.axis_index("mp")
+        total = self.part[me].astype(F32)
+        for k in range(1, self.n):
+            total += self.slots[k - 1].astype(F32)
+        self.full[me] = total.astype(BF)
+        self.second = spread(
+            self.n, lambda peer: self.full.at[me], lambda k: self.full.at[me],
+            self.sems.at[2], self.sems.at[3],
+        )
+
+    def done(self):
+        finish(self.second)
+
+
+def main_kernel(
+    n, kv_count, repeats,
+    hid, que, key, val, ctx, seg, downq, upq_h, downv, upv_h, ids, ids_v, bank,
+    feats,
+    h_v, q_v, c_v, k_v, v_v, dn, upq, upv, mask, vsum, dq_t, vg, sums, grads0,
+    low_part, low_slots, low_full, back_part, back_slots, back_full, sems, links,
 ):
     m = lax.axis_index("mp")
     heads = kv_count * repeats
     kv_first = m * heads // (H // KVH)
     kv_cols = pl.ds(pl.multiple_of(kv_first * DH, DH), kv_count * DH)
-    cands = que.shape[0]
+    cands, seq, width = que.shape
     count = [0]
 
     def load(src, dst):
@@ -106,27 +168,85 @@
         copy.start()
         return copy
 
+    early = [load(downq, dn.at[:, :R]), load(downv, dn.at[:, R:])]
+    early += [load(hid.at[b], h_v.at[b]) for b in range(cands)]
     kv_copies = [load(key.at[:, :, kv_cols], k_v), load(val.at[:, :, kv_cols], v_v)]
     tok = [[load(que.at[b], q_v.at[b]), load(ctx.at[b], c_v.at[b])] for b in range(cands)]
-    late = [load(hid.at[b], h_v.at[b]) for b in range(cands)]
-    late += [load(downq, dn.at[:, :R]), load(downv, dn.at[:, R:]), load(upq_h, upq)]
-    late += [load(upv_h.at[:, kv_cols], upv)]
-    for copy in kv_copies:
-        copy.wait()
+    late = [load(upq_h, upq), load(upv_h.at[:, kv_cols], upv)]
+
+    build_mask(seg, mask, 0)
+    finish(early)
+    for c in range(cands):
+        low = dot(h_v[c], dn[...]).astype(BF)
+        low_part[:, c] = low.reshape(n, seq // n, 2 * R)
+    meet(n)
+    low_sum = Reduce(n, low_part, low_slots, low_full, links.at[0])
+    low_sum.scatter()
+    finish(kv_copies)
+    pending = low_sum
     for b in range(cands):
-        build_mask(seg, mask, b)
-        for copy in tok[b]:
-            copy.wait()
+        if b:
+            build_mask(seg, mask, b)
+        finish(tok[b])
         for g in range(kv_count):
             attend(b, g, repeats, q_v, c_v, k_v, v_v, mask, vsum, dq_t, vg)
+            if g == 0:
+                pending.gather()
         if b == 0:
-            for copy in late:
-                copy.wait()
-            for c in range(cands):
-                low[c] = dot(h_v[c], dn[...]).astype(BF)
+            finish(late)
         back_q, back_v = back_partial(b, kv_count, upq, upv, dq_t, vg)
-        back[b, :R, :] = back_q.astype(BF)
-        back[b, R:, :] = back_v.astype(BF)
+        back = jnp.concatenate([back_q, back_v], axis=0).astype(BF)
+        pending.done()
+        back_part[b] = back.reshape(n, 2 * R // n, seq)
+        pending = Reduce(
+            n, back_part.at[b], back_slots.at[b], back_full.at[b], links.at[b + 1]
+        )
+        pending.scatter()
+    low = [low_full[:, b].reshape(seq, 2 * R) for b in range(cands)]
+    sums[...] = jnp.zeros_like(sums)
+    add_upq(sums, ids, dq_t, low)
+    pending.gather()
+    add_upv(sums, ids_v, vg, low)
+    for b in range(cands - 1):
+        whole = back_full[b].reshape(2 * R, seq)
+        for lo in range(0, width, 512):
+            cols = slice(lo, lo + 512)
+            grads0[b, :, cols] = dot(whole, h_v[b, :, cols]).astype(BF)
+    pending.done()
+    add_down(sums, ids, h_v, grads0, back_full[cands - 1].reshape(2 * R, seq))
+    rows = KB // n
+    for b in range(cands):
+        feats[:, b] = project(sums, bank, b).reshape(n, rows, PB)
+
+
+def tail_kernel(n, feats, seeds, out, slots, pack, slots2, links):
+    me = lax.axis_index("mp")
+    cands, rows = feats.shape[1], feats.shape[2]
+    outs = out.shape[1]
+    meet(n)
+    first = spread(n, lambda peer: feats.at[peer], lambda k: slots.at[k - 1], links.at[0], links.at[1])
+    finish(first)
+    total = feats[me]
+    for k in range(1, n):
+        total += slots[k - 1]
+    flat = jnp.concatenate(
+        [
+            jnp.concatenate([total[b, i : i + 1] for i in range(rows)], axis=1)
+            for b in range(cands)
+        ],
+        axis=0,
+    )
+    square = jnp.sum(flat * flat, axis=1, keepdims=True)
+    number = dot_nt(flat.astype(BF), seeds[...])
+    for j in range(n):
+        pack[j, :, :outs] = number[:, j * outs : (j + 1) * outs]
+        pack[j, :, outs:] = jnp.broadcast_to(square, (cands, outs))
+    second = spread(n, lambda peer: pack.at[peer], lambda k: slots2.at[k - 1], links.at[2], links.at[3])
+    finish(second)
+    both = pack[me]
+    for k in range(1, n):
+        both += slots2[k - 1]
+    out[...] = both[:, :outs] * lax.rsqrt(both[:, outs:] / K + EPS) * K ** (-0.5)
 
 
 CHUNK = 256
@@ -145,7 +265,7 @@
 
     def step(i, carry):
         rows = pl.ds(pl.multiple_of(i * chunk, chunk), chunk)
-        grads = [dot(dq_t[b, rows, :], low[b, :, :R]) for b in range(cands)]
+        grads = [dot(dq_t[b, rows, :], low[b][:, :R]) for b in range(cands)]
         bucket_add(sums, ids[2:3, rows], jnp.concatenate(grads, axis=1).astype(BF), False)
         return carry
 
@@ -154,17 +274,18 @@
 
 def add_upv(sums, ids, vg, low):
     cands, width = vg.shape[0], vg.shape[2]
-    grads = [dot(vg[b].T, low[b, :, R:]) for b in range(cands)]
+    grads = [dot(vg[b].T, low[b][:, R:]) for b in range(cands)]
     bucket_add(sums, ids[...], jnp.concatenate(grads, axis=1).astype(BF), False)
 
 
-def add_down(sums, ids, h_v, back):
+def add_down(sums, ids, h_v, grads0, back):
     cands, width = h_v.shape[0], h_v.shape[2]
     chunk = min(CHUNK, width)
 
     def step(i, carry):
         cols = pl.ds(pl.multiple_of(i * chunk, chunk), chunk)
-        grads = [dot(back[b], h_v[b, :, cols]).astype(BF) for b in range(cands)]
+        grads = [grads0[b, :, cols] for b in range(cands - 1)]
+        grads.append(dot(back, h_v[cands - 1, :, cols]).astype(BF))
         for j in range(2):
             part = jnp.concatenate([grad[j * R : (j + 1) * R] for grad in grads], axis=0)
             bucket_add(sums, ids[j : j + 1, cols], part, True)
@@ -179,15 +300,6 @@
         part = sums[t * KB : (t + 1) * KB, b * R : (b + 1) * R].astype(BF)
         total += dot(part, bank[t])
     return total
-
-
-def feature_kernel(hid, dq_t, vg, low, back, ids, ids_v, bank, feats, sums):
-    sums[...] = jnp.zeros_like(sums)
-    add_upq(sums, ids, dq_t, low)
-    add_upv(sums, ids_v, vg, low)
-    add_down(sums, ids, hid, back)
-    for b in range(hid.shape[0]):
-        feats[b] = project(sums, bank, b).astype(BF)
 
 
 ANY = pl.BlockSpec(memory_space=pl.ANY)
@@ -208,16 +320,14 @@
     seeds_all = lax.all_gather(seed_feats, "dp", axis=0, tiled=True)
     ids = tile_rows * KB + block_rows
     ids_v = lax.dynamic_slice_in_dim(tile_value * KB + block_value, kv_first * DH, kvw, 0)[None]
-    dq_t, vg, low, back = pl.pallas_call(
-        functools.partial(attention_kernel, kv_count, repeats),
-        out_shape=(
-            jax.ShapeDtypeStruct((cands, width, seq), BF),
-            jax.ShapeDtypeStruct((cands, seq, kvw), BF),
-            jax.ShapeDtypeStruct((cands, seq, 2 * R), BF),
-            jax.ShapeDtypeStruct((cands, 2 * R, seq), BF),
-        ),
-        in_specs=[ANY] * 5 + [VMEM] + [ANY] * 4,
-        out_specs=(VMEM,) * 4,
+    n = lax.axis_size("mp")
+    hop = [pltpu.VMEM((n, cands, seq // n, 2 * R), BF), pltpu.VMEM((n - 1, cands, seq // n, 2 * R), BF)]
+    fold = (2 * R // n, seq)
+    feats = pl.pallas_call(
+        functools.partial(main_kernel, n, kv_count, repeats),
+        out_shape=jax.ShapeDtypeStruct((n, cands, KB // n, PB), F32),
+        in_specs=[ANY] * 5 + [VMEM] + [ANY] * 4 + [VMEM] * 3,
+        out_specs=VMEM,
         scratch_shapes=[
             pltpu.VMEM((cands, seq, width), BF),
             pltpu.VMEM((cands, seq, width), BF),
@@ -229,39 +339,42 @@
             pltpu.VMEM((R, kvw), BF),
             pltpu.VMEM((seq, seq), F32),
             pltpu.VMEM((seq, DH), F32),
+            pltpu.VMEM((cands, width, seq), BF),
+            pltpu.VMEM((cands, seq, kvw), BF),
+            pltpu.VMEM((KB * NT, cands * R), F32),
+            pltpu.VMEM((max(cands - 1, 1), 2 * R, width), BF),
+            hop[0], hop[1], hop[0],
+            pltpu.VMEM((cands, n) + fold, BF),
+            pltpu.VMEM((cands, n - 1) + fold, BF),
+            pltpu.VMEM((cands, n) + fold, BF),
             pltpu.SemaphoreType.DMA((6 + 3 * cands,)),
+            pltpu.SemaphoreType.DMA((cands + 1, 4, n - 1)),
         ],
-        compiler_params=pltpu.CompilerParams(vmem_limit_bytes=56 << 20),
+        compiler_params=pltpu.CompilerParams(
+            vmem_limit_bytes=56 << 20, collective_id=0, has_side_effects=True
+        ),
         cost_estimate=pl.CostEstimate(
-            flops=cands * heads * seq * seq * DH * 8, bytes_accessed=16 << 20,
+            flops=cands * heads * seq * seq * DH * 12, bytes_accessed=16 << 20,
             transcendentals=cands * heads * seq * seq,
         ),
-        name="attention",
+        name="gradient_features",
     )(hidden_in, query_act, key_act, value_act, ctx_grad, segment_ids,
-      down_query, up_query, down_value, up_value)
-    low, back = lax.psum((low, back), "mp")
-    feats = pl.pallas_call(
-        feature_kernel,
-        out_shape=jax.ShapeDtypeStruct((cands, KB, PB), BF),
-        in_specs=[VMEM] * 8,
+      down_query, up_query, down_value, up_value, ids, ids_v, tile_bank)
+    outs = seeds_all.shape[0] // n
+    return pl.pallas_call(
+        functools.partial(tail_kernel, n),
+        out_shape=jax.ShapeDtypeStruct((cands, outs), F32),
+        in_specs=[VMEM] * 2,
         out_specs=VMEM,
-        scratch_shapes=[pltpu.VMEM((KB * NT, cands * R), F32)],
-        compiler_params=pltpu.CompilerParams(vmem_limit_bytes=56 << 20),
-        cost_estimate=pl.CostEstimate(
-            flops=cands * seq * width * R * 8, bytes_accessed=8 << 20, transcendentals=0
-        ),
-        name="features",
-    )(hidden_in, dq_t, vg, low, back, ids, ids_v, tile_bank)
-    feat_slice = lax.psum_scatter(
-        feats.reshape(cands, K), "mp", scatter_dimension=1, tiled=True
-    ).astype(F32)
-    feat_square = jnp.sum(feat_slice * feat_slice, axis=1)
-    partial_value = jnp.einsum(
-        "bk,sk->bs", feat_slice.astype(BF), seeds_all, preferred_element_type=F32
-    )
-    total_square = lax.psum(feat_square, "mp")
-    numerator = lax.psum_scatter(partial_value, "mp", scatter_dimension=1, tiled=True)
-    return numerator * lax.rsqrt(total_square / K + EPS)[:, None] * K ** (-0.5)
+        scratch_shapes=[
+            pltpu.VMEM((n - 1, cands, KB // n, PB), F32),
+            pltpu.VMEM((n, cands, 2 * outs), F32),
+            pltpu.VMEM((n - 1, cands, 2 * outs), F32),
+            pltpu.SemaphoreType.DMA((4, n - 1)),
+        ],
+        compiler_params=pltpu.CompilerParams(collective_id=1, has_side_effects=True),
+        name="seed_scores",
+    )(feats, seeds_all)
 
 
 def solution(mesh):

time: 207 us -> 92.4 us (0.45)
  waiting for transfers between devices: 113 us -> 0.73 us
  Pallas kernels: 60.4 us -> 74 us
  blocking collectives: 8.92 us -> 0 us
  local copies, waits for them, and re-layouts: 5.32 us -> 1.87 us
  matrix products: 2.48 us -> 0 us
    unnamed x6 -> x1, waiting for transfers between devices: 59.2 us -> 0.71 us
    psum x1 -> x0, waiting for transfers between devices: 54.2 us -> none  [local(): low, back = lax.psum((low, back), 'mp')]
    pallas_call x2, Pallas kernels: 60.4 us -> 74 us  [the longest x1 62.8 us: local(): pl.pallas_call(functools.partial(main_kernel, n, kv_count, repeats), out_...]
    psum x1 -> x0, blocking collectives: 8.92 us -> none  [local(): total_square = lax.psum(feat_square, 'mp')]
    unnamed x11 -> x1, local copies, waits for them, and re-layouts: 4.68 us -> 1.23 us
    unnamed x1 -> x0, matrix products: 2.48 us -> none
  transfers between devices with their start and end apart: 4 -> 1, of which waited for: 3 -> 0; matrix products, arithmetic and copies ran while one was open for 1% -> 3% of each run, Pallas kernels for 0% -> 68%
where the time goes in v1:
time: 92.4 us; the launch traced here: 92.2 us
  Pallas kernels  74 us (80%)
  between operations  13.4 us (15%)
  other arithmetic  2.11 us (2%)
  local copies, waits for them, and re-layouts  1.87 us (2%)
    pallas_call x1, Pallas kernels, local(): pl.pallas_call(functools.partial(main_kernel, n, kv_count, repeats), out_...  62.8 us
    pallas_call x1, Pallas kernels, local(): pl.pallas_call(functools.partial(tail_kernel, n), out_shape=jax.ShapeDtyp...  11.2 us
  transfers between devices with their start and end apart: 1, of which 0 were waited for; matrix products, arithmetic and copies ran while one was open for 3% of the time, Pallas kernels for 68%

profile of v1, /device:TPU:0, one launch (start us, length us, event | category | flops | bytes accessed | tf_op | source)
XLA Modules:
  0.0 92.2 jit_solution(8213998487332294495)
XLA Ops:
  6.5 0.0 all-gather.2.cloned.1.call-start
  6.5 0.7 all-gather.2.cloned.1.call-update
  7.3 0.7 multiply_add_fusion.1
  8.0 0.6 dynamic_slice.3
  8.6 1.4 %multiply_add_fusion.ids = s32[3,2048]{1,0:T(4,128)} fusion(s32[3,2048]{1,0:T(4,128)} %param.26, s32[3,2048]{1,0:T(4,128)} %param.27), kind=kLoop, calls=%fused_computation | loop fusion | flops 12288 | bytes 73728 | tf_op jit(solution)/shard_map/add | solution.py:321
  10.0 62.8 %gradient_features.1.feats = f32[4,2,16,128]{3,2,1,0:T(8,128)} custom-call(bf16[2,512,2048]{2,1,0:T(8,128)(2,1)} %hid.1, bf16[2,512,2048]{2,1,0:T(8,128)(2,1)} %que.1, bf16[2,512,1024]{2,1,0:T(8,128)(2,1)} %key.1, bf16[2,512,1024]{2,1,0:T(8,128)(2,1)} %val.1, bf16[2,512,2048]{2,1,0:T(8,128)(2,1)} %ctx.1, s32[2,512]{1,0:T(2,128)} %seg.1, ...), custom_call_target="tpu_custom_call" | custom-call | flops 12884901888 | bytes 16777216 | tf_op jit(solution)/shard_map/gradient_features/pallas_call | solution.py:326
  72.8 0.0 all-gather.2.cloned.1.call-done.seeds
  72.9 11.2 %seed_scores.1 = f32[2,64]{1,0:T(2,128)} custom-call(f32[4,2,16,128]{3,2,1,0:T(8,128)} %gradient_features.1.feats, bf16[256,2048]{1,0:T(8,128)(2,1)} %all-gather.2.cloned.1.call-done.seeds), custom_call_target="tpu_custom_call" | custom-call | tf_op jit(solution)/shard_map/seed_scores/pallas_call | solution.py:364
  84.1 1.2 %copy.18 = f32[2,64]{1,0:T(2,128)} copy(f32[2,64]{1,0:T(2,128)} %seed_scores.1) | data formatting | bytes 1024
Async XLA Ops:
  6.5 66.3 %all-gather.2.cloned.1.call-start = ((), (), s32[]{:S(2)}) async-start(), calls=%async_computation | async-start | bytes 1179648 | tf_op jit(solution)/shard_map/all_gather | solution.py:320
Sparse Core Ops, SparseCore 0:
  9.0 24.8 all-gather.1

commit v2 on v1

--- a/solution.py
+++ b/solution.py
@@ -45,6 +45,9 @@
         mask_ref[:, lo : lo + REACH] = jnp.where(allowed, 0.0, NEG)
 
 
+UNROLL = 4
+
+
 def attend(b, g, repeats, q_v, c_v, k_v, v_v, mask, vsum, dq_t, vg):
     seq = mask.shape[0]
     kv_cols = slice(g * DH, (g + 1) * DH)
@@ -54,27 +57,64 @@
     scale = 1.0 / math.sqrt(DH)
     vsum[...] = jnp.zeros_like(vsum)
 
-    def head(h, carry):
-        cols = pl.ds(pl.multiple_of((g * repeats + h) * DH, DH), DH)
+    units = [(j, lo) for j in range(UNROLL) for lo in range(0, seq, REACH)]
+
+    def heads(i, carry):
+        cols = [
+            pl.ds(pl.multiple_of((g * repeats + i * UNROLL + j) * DH, DH), DH)
+            for j in range(UNROLL)
+        ]
+
+        def span(lo):
+            return slice(max(lo - REACH, 0), lo + REACH)
+
+        def products(j, lo):
+            quer = q_v[b, lo : lo + REACH, cols[j]]
+            cot = c_v[b, lo : lo + REACH, cols[j]]
+            return dot_nt(keys[span(lo)], quer), dot_nt(vals[span(lo)], cot)
+
+        def soft(lo, logits, prob_grads):
+            first, last = span(lo).start, span(lo).stop
+            probs, grads = [], []
+            for at in range(lo, lo + REACH, DH):
+                low, high = max(at - REACH, 0), at + DH
+                rows, lanes = slice(low - first, high - first), slice(at - lo, at - lo + DH)
+                logit = logits[rows, lanes] + mask[low:high, at : at + DH]
+                prob_grad = prob_grads[rows, lanes]
+                top = jnp.max(logit, axis=0, keepdims=True)
+                terms = jnp.exp2((logit - top) * (scale * math.log2(math.e)))
+                prob = terms * (1.0 / jnp.sum(terms, axis=0, keepdims=True))
+                delta = jnp.sum(prob * prob_grad, axis=0, keepdims=True)
+
+                def padded(block):
+                    above = jnp.zeros((low - first, DH), BF)
+                    below = jnp.zeros((last - high, DH), BF)
+                    parts = [p for p in (above, block.astype(BF), below) if p.shape[0]]
+                    return jnp.concatenate(parts, axis=0) if len(parts) > 1 else parts[0]
+
+                probs.append(padded(prob))
+                grads.append(padded(prob * (prob_grad - delta)))
+            return jnp.concatenate(probs, axis=1), jnp.concatenate(grads, axis=1)
+
+        held = {}
+        ready = products(*units[0])
+        for at, (j, lo) in enumerate(units):
+            logits, prob_grads = ready
+            if at + 1 < len(units):
+                ready = products(*units[at + 1])
+            probs, grads = soft(lo, logits, prob_grads)
+            held[j, lo] = probs
+            dq = dot(keys_t[:, span(lo)], grads) * scale
+            dq_t[b, cols[j], lo : lo + REACH] = dq.astype(BF)
         for lo in range(0, seq, REACH):
-            first = max(lo - REACH, 0)
-            rows = slice(first, lo + REACH)
-            quer = q_v[b, lo : lo + REACH, cols]
-            cot = c_v[b, lo : lo + REACH, cols]
-            logit = dot_nt(keys[rows], quer) + mask[rows, lo : lo + REACH]
-            prob_grad = dot_nt(vals[rows], cot)
-            top = jnp.max(logit, axis=0, keepdims=True)
-            terms = jnp.exp2((logit - top) * (scale * math.log2(math.e)))
-            inv = 1.0 / jnp.sum(terms, axis=0, keepdims=True)
-            probs = terms * inv
-            delta = jnp.sum(probs * prob_grad, axis=0, keepdims=True)
-            logit_grad = (probs * (prob_grad - delta)).astype(BF)
-            vsum[rows, :] += dot(probs.astype(BF), cot)
-            dq = dot(keys_t[:, rows], logit_grad) * scale
-            dq_t[b, cols, lo : lo + REACH] = dq.astype(BF)
+            probs = jnp.concatenate([held[j, lo] for j in range(UNROLL)], axis=1)
+            cots = jnp.concatenate(
+                [c_v[b, lo : lo + REACH, cols[j]] for j in range(UNROLL)], axis=0
+            )
+            vsum[span(lo), :] += dot(probs, cots)
         return carry
 
-    lax.fori_loop(0, repeats, head, 0)
+    lax.fori_loop(0, repeats // UNROLL, heads, 0)
     vg[b, :, kv_cols] = vsum[...].astype(BF)
 
 
@@ -150,9 +190,10 @@
 
 def main_kernel(
     n, kv_count, repeats,
-    hid, que, key, val, ctx, seg, downq, upq_h, downv, upv_h, ids, ids_v, bank,
+    hid, que, key, val, ctx, seg, downq, upq_h, downv, upv_h,
+    block, tile, block_v, tile_v, bank,
     feats,
-    h_v, q_v, c_v, k_v, v_v, dn, upq, upv, mask, vsum, dq_t, vg, sums, grads0,
+    h_v, q_v, c_v, k_v, v_v, dn, upq, upv, mask, vsum, dq_t, vg, sums, grads0, ids_s,
     low_part, low_slots, low_full, back_part, back_slots, back_full, sems, links,
 ):
     m = lax.axis_index("mp")
@@ -175,8 +216,9 @@
     late = [load(upq_h, upq), load(upv_h.at[:, kv_cols], upv)]
 
     build_mask(seg, mask, 0)
-    finish(early)
+    finish(early[:2])
     for c in range(cands):
+        early[2 + c].wait()
         low = dot(h_v[c], dn[...]).astype(BF)
         low_part[:, c] = low.reshape(n, seq // n, 2 * R)
     meet(n)
@@ -204,7 +246,10 @@
         pending.scatter()
     low = [low_full[:, b].reshape(seq, 2 * R) for b in range(cands)]
     sums[...] = jnp.zeros_like(sums)
-    add_upq(sums, ids, dq_t, low)
+    ids = tile[...] * KB + block[...]
+    ids_v = tile_v[:, kv_cols] * KB + block_v[:, kv_cols]
+    ids_s[...] = ids
+    add_upq(sums, ids_s, dq_t, low)
     pending.gather()
     add_upv(sums, ids_v, vg, low)
     for b in range(cands - 1):
@@ -213,7 +258,7 @@
             cols = slice(lo, lo + 512)
             grads0[b, :, cols] = dot(whole, h_v[b, :, cols]).astype(BF)
     pending.done()
-    add_down(sums, ids, h_v, grads0, back_full[cands - 1].reshape(2 * R, seq))
+    add_down(sums, ids_s, h_v, grads0, back_full[cands - 1].reshape(2 * R, seq))
     rows = KB // n
     for b in range(cands):
         feats[:, b] = project(sums, bank, b).reshape(n, rows, PB)
@@ -275,7 +320,7 @@
 def add_upv(sums, ids, vg, low):
     cands, width = vg.shape[0], vg.shape[2]
     grads = [dot(vg[b].T, low[b][:, R:]) for b in range(cands)]
-    bucket_add(sums, ids[...], jnp.concatenate(grads, axis=1).astype(BF), False)
+    bucket_add(sums, ids, jnp.concatenate(grads, axis=1).astype(BF), False)
 
 
 def add_down(sums, ids, h_v, grads0, back):
@@ -316,17 +361,14 @@
     kv_count = max(heads // (H // KVH), 1)
     repeats = heads // kv_count
     kvw = kv_count * DH
-    kv_first = lax.axis_index("mp") * heads // (H // KVH)
     seeds_all = lax.all_gather(seed_feats, "dp", axis=0, tiled=True)
-    ids = tile_rows * KB + block_rows
-    ids_v = lax.dynamic_slice_in_dim(tile_value * KB + block_value, kv_first * DH, kvw, 0)[None]
     n = lax.axis_size("mp")
     hop = [pltpu.VMEM((n, cands, seq // n, 2 * R), BF), pltpu.VMEM((n - 1, cands, seq // n, 2 * R), BF)]
     fold = (2 * R // n, seq)
     feats = pl.pallas_call(
         functools.partial(main_kernel, n, kv_count, repeats),
         out_shape=jax.ShapeDtypeStruct((n, cands, KB // n, PB), F32),
-        in_specs=[ANY] * 5 + [VMEM] + [ANY] * 4 + [VMEM] * 3,
+        in_specs=[ANY] * 5 + [VMEM] + [ANY] * 4 + [VMEM] * 5,
         out_specs=VMEM,
         scratch_shapes=[
             pltpu.VMEM((cands, seq, width), BF),
@@ -343,6 +385,7 @@
             pltpu.VMEM((cands, seq, kvw), BF),
             pltpu.VMEM((KB * NT, cands * R), F32),
             pltpu.VMEM((max(cands - 1, 1), 2 * R, width), BF),
+            pltpu.VMEM(block_rows.shape, jnp.int32),
             hop[0], hop[1], hop[0],
             pltpu.VMEM((cands, n) + fold, BF),
             pltpu.VMEM((cands, n - 1) + fold, BF),
@@ -359,7 +402,8 @@
         ),
         name="gradient_features",
     )(hidden_in, query_act, key_act, value_act, ctx_grad, segment_ids,
-      down_query, up_query, down_value, up_value, ids, ids_v, tile_bank)
+      down_query, up_query, down_value, up_value,
+      block_rows, tile_rows, block_value[None], tile_value[None], tile_bank)
     outs = seeds_all.shape[0] // n
     return pl.pallas_call(
         functools.partial(tail_kernel, n),

time: 92.4 us -> 76.4 us (0.83)
  Pallas kernels: 74 us -> 60.8 us
  other arithmetic: 2.11 us -> 0 us
    pallas_call x1, Pallas kernels: 62.8 us -> 50.3 us  [local(): pl.pallas_call(functools.partial(main_kernel, n, kv_count, repeats), out_...]
    add x2 -> x0, other arithmetic: 2.11 us -> none  [the longest x1 1.4 us: local(): ids = tile_rows * KB + block_rows]
  transfers between devices with their start and end apart: 1 -> 1, of which waited for: 0 -> 0; matrix products, arithmetic and copies ran while one was open for 3% -> 0% of each run, Pallas kernels for 68% -> 66%
where the time goes in v2:
time: 76.4 us; the launch traced here: 76.2 us
  Pallas kernels  60.8 us (80%)
  between operations  13.4 us (18%)
  local copies, waits for them, and re-layouts  1.23 us (2%)
    pallas_call x1, Pallas kernels, local(): pl.pallas_call(functools.partial(main_kernel, n, kv_count, repeats), out_...  50.3 us
    pallas_call x1, Pallas kernels, local(): pl.pallas_call(functools.partial(tail_kernel, n), out_shape=jax.ShapeDtyp...  10.5 us
  transfers between devices with their start and end apart: 1, of which 0 were waited for; matrix products, arithmetic and copies ran while one was open for 0% of the time, Pallas kernels for 66%

profile of v2, /device:TPU:0, one launch (start us, length us, event | category | flops | bytes accessed | tf_op | source)
XLA Modules:
  0.0 76.2 jit_solution(5470560084852993997)
XLA Ops:
  6.5 0.0 all-gather.2.cloned.1.call-start
  6.5 0.7 all-gather.2.cloned.1.call-update
  7.3 50.3 %gradient_features.1.feats = f32[4,2,16,128]{3,2,1,0:T(8,128)} custom-call(bf16[2,512,2048]{2,1,0:T(8,128)(2,1)} %hid.1, bf16[2,512,2048]{2,1,0:T(8,128)(2,1)} %que.1, bf16[2,512,1024]{2,1,0:T(8,128)(2,1)} %key.1, bf16[2,512,1024]{2,1,0:T(8,128)(2,1)} %val.1, bf16[2,512,2048]{2,1,0:T(8,128)(2,1)} %ctx.1, s32[2,512]{1,0:T(2,128)} %seg.1, ...), custom_call_target="tpu_custom_call" | custom-call | flops 12884901888 | bytes 16777216 | tf_op jit(solution)/shard_map/gradient_features/pallas_call | solution.py:368
  57.6 0.0 all-gather.2.cloned.1.call-done.seeds
  57.6 10.5 %seed_scores.1 = f32[2,64]{1,0:T(2,128)} custom-call(f32[4,2,16,128]{3,2,1,0:T(8,128)} %gradient_features.1.feats, bf16[256,2048]{1,0:T(8,128)(2,1)} %all-gather.2.cloned.1.call-done.seeds), custom_call_target="tpu_custom_call" | custom-call | tf_op jit(solution)/shard_map/seed_scores/pallas_call | solution.py:408
  68.1 1.2 %copy.18 = f32[2,64]{1,0:T(2,128)} copy(f32[2,64]{1,0:T(2,128)} %seed_scores.1) | data formatting | bytes 1024
Async XLA Ops:
  6.5 51.1 %all-gather.2.cloned.1.call-start = ((), (), s32[]{:S(2)}) async-start(), calls=%async_computation | async-start | bytes 1179648 | tf_op jit(solution)/shard_map/all_gather | solution.py:364
Sparse Core Ops, SparseCore 0:
  9.0 24.8 all-gather.1

commit v3 on v2

--- a/solution.py
+++ b/solution.py
@@ -130,17 +130,24 @@
 MESH = pl.DeviceIdType.MESH
 
 
-def meet(n):
+def device(axis, peer):
+    if axis == "dp":
+        return (peer, lax.axis_index("mp"))
+    return (lax.axis_index("dp"), peer)
+
+
+def meet(sizes):
     barrier = pltpu.get_barrier_semaphore()
-    me = lax.axis_index("mp")
-    for k in range(1, n):
-        peer = (lax.axis_index("dp"), lax.rem(me + k, n))
-        pl.semaphore_signal(barrier, inc=1, device_id=peer, device_id_type=MESH)
-    pl.semaphore_wait(barrier, n - 1)
-
-
-def spread(n, source, target, send, recv):
-    me = lax.axis_index("mp")
+    for axis, n in sizes:
+        me = lax.axis_index(axis)
+        for k in range(1, n):
+            peer = device(axis, lax.rem(me + k, n))
+            pl.semaphore_signal(barrier, inc=1, device_id=peer, device_id_type=MESH)
+    pl.semaphore_wait(barrier, sum(n - 1 for _, n in sizes))
+
+
+def spread(axis, n, source, target, send, recv):
+    me = lax.axis_index(axis)
     copies = []
     for k in range(1, n):
         peer = lax.rem(me + k, n)
@@ -149,7 +156,7 @@
             dst_ref=target(k),
             send_sem=send.at[k - 1],
             recv_sem=recv.at[k - 1],
-            device_id=(lax.axis_index("dp"), peer),
+            device_id=device(axis, peer),
             device_id_type=MESH,
         )
         copy.start()
@@ -168,7 +175,7 @@
 
     def scatter(self):
         self.first = spread(
-            self.n, lambda peer: self.part.at[peer], lambda k: self.slots.at[k - 1],
+            "mp", self.n, lambda peer: self.part.at[peer], lambda k: self.slots.at[k - 1],
             self.sems.at[0], self.sems.at[1],
         )
 
@@ -180,7 +187,7 @@
             total += self.slots[k - 1].astype(F32)
         self.full[me] = total.astype(BF)
         self.second = spread(
-            self.n, lambda peer: self.full.at[me], lambda k: self.full.at[me],
+            "mp", self.n, lambda peer: self.full.at[me], lambda k: self.full.at[me],
             self.sems.at[2], self.sems.at[3],
         )
 
@@ -189,12 +196,13 @@
 
 
 def main_kernel(
-    n, kv_count, repeats,
+    n, dp, kv_count, repeats,
     hid, que, key, val, ctx, seg, downq, upq_h, downv, upv_h,
-    block, tile, block_v, tile_v, bank,
-    feats,
+    block, tile, block_v, tile_v, bank, seeds,
+    out,
     h_v, q_v, c_v, k_v, v_v, dn, upq, upv, mask, vsum, dq_t, vg, sums, grads0, ids_s,
-    low_part, low_slots, low_full, back_part, back_slots, back_full, sems, links,
+    low_part, low_slots, low_full, back_part, back_slots, back_full,
+    feats, feat_slots, pack, pack_slots, seeds_all, sems, links, seed_links,
 ):
     m = lax.axis_index("mp")
     heads = kv_count * repeats
@@ -216,14 +224,19 @@
     late = [load(upq_h, upq), load(upv_h.at[:, kv_cols], upv)]
 
     build_mask(seg, mask, 0)
+    spot = lax.axis_index("dp")
+    seeds_all[spot] = seeds[...]
+    meet((("mp", n), ("dp", dp)))
     finish(early[:2])
     for c in range(cands):
         early[2 + c].wait()
         low = dot(h_v[c], dn[...]).astype(BF)
         low_part[:, c] = low.reshape(n, seq // n, 2 * R)
-    meet(n)
     low_sum = Reduce(n, low_part, low_slots, low_full, links.at[0])
     low_sum.scatter()
+    seed_copies = spread(
+        "dp", dp, lambda peer: seeds, lambda k: seeds_all.at[spot], seed_links.at[0], seed_links.at[1]
+    )
     finish(kv_copies)
     pending = low_sum
     for b in range(cands):
@@ -262,18 +275,13 @@
     rows = KB // n
     for b in range(cands):
         feats[:, b] = project(sums, bank, b).reshape(n, rows, PB)
-
-
-def tail_kernel(n, feats, seeds, out, slots, pack, slots2, links):
-    me = lax.axis_index("mp")
-    cands, rows = feats.shape[1], feats.shape[2]
-    outs = out.shape[1]
-    meet(n)
-    first = spread(n, lambda peer: feats.at[peer], lambda k: slots.at[k - 1], links.at[0], links.at[1])
-    finish(first)
-    total = feats[me]
+    tail = links.at[cands + 1]
+    finish(spread(
+        "mp", n, lambda peer: feats.at[peer], lambda k: feat_slots.at[k - 1], tail.at[0], tail.at[1]
+    ))
+    total = feats[m]
     for k in range(1, n):
-        total += slots[k - 1]
+        total += feat_slots[k - 1]
     flat = jnp.concatenate(
         [
             jnp.concatenate([total[b, i : i + 1] for i in range(rows)], axis=1)
@@ -282,16 +290,19 @@
         axis=0,
     )
     square = jnp.sum(flat * flat, axis=1, keepdims=True)
-    number = dot_nt(flat.astype(BF), seeds[...])
+    finish(seed_copies)
+    outs = pack.shape[2] // 2
+    number = dot_nt(flat.astype(BF), seeds_all[...].reshape(n * outs, rows * PB))
     for j in range(n):
         pack[j, :, :outs] = number[:, j * outs : (j + 1) * outs]
         pack[j, :, outs:] = jnp.broadcast_to(square, (cands, outs))
-    second = spread(n, lambda peer: pack.at[peer], lambda k: slots2.at[k - 1], links.at[2], links.at[3])
-    finish(second)
-    both = pack[me]
+    finish(spread(
+        "mp", n, lambda peer: pack.at[peer], lambda k: pack_slots.at[k - 1], tail.at[2], tail.at[3]
+    ))
+    both = pack[m]
     for k in range(1, n):
-        both += slots2[k - 1]
-    out[...] = both[:, :outs] * lax.rsqrt(both[:, outs:] / K + EPS) * K ** (-0.5)
+        both += pack_slots[k - 1]
+    out[...] = both
 
 
 CHUNK = 256
@@ -361,14 +372,14 @@
     kv_count = max(heads // (H // KVH), 1)
     repeats = heads // kv_count
     kvw = kv_count * DH
-    seeds_all = lax.all_gather(seed_feats, "dp", axis=0, tiled=True)
-    n = lax.axis_size("mp")
+    n, dp = lax.axis_size("mp"), lax.axis_size("dp")
+    outs = seed_feats.shape[0] * dp // n
     hop = [pltpu.VMEM((n, cands, seq // n, 2 * R), BF), pltpu.VMEM((n - 1, cands, seq // n, 2 * R), BF)]
     fold = (2 * R // n, seq)
-    feats = pl.pallas_call(
-        functools.partial(main_kernel, n, kv_count, repeats),
-        out_shape=jax.ShapeDtypeStruct((n, cands, KB // n, PB), F32),
-        in_specs=[ANY] * 5 + [VMEM] + [ANY] * 4 + [VMEM] * 5,
+    both = pl.pallas_call(
+        functools.partial(main_kernel, n, dp, kv_count, repeats),
+        out_shape=jax.ShapeDtypeStruct((cands, 2 * outs), F32),
+        in_specs=[ANY] * 5 + [VMEM] + [ANY] * 4 + [VMEM] * 6,
         out_specs=VMEM,
         scratch_shapes=[
             pltpu.VMEM((cands, seq, width), BF),
@@ -390,8 +401,14 @@
             pltpu.VMEM((cands, n) + fold, BF),
             pltpu.VMEM((cands, n - 1) + fold, BF),
             pltpu.VMEM((cands, n) + fold, BF),
+            pltpu.VMEM((n, cands, KB // n, PB), F32),
+            pltpu.VMEM((n - 1, cands, KB // n, PB), F32),
+            pltpu.VMEM((n, cands, 2 * outs), F32),
+            pltpu.VMEM((n - 1, cands, 2 * outs), F32),
+            pltpu.VMEM((dp,) + seed_feats.shape, BF),
             pltpu.SemaphoreType.DMA((6 + 3 * cands,)),
-            pltpu.SemaphoreType.DMA((cands + 1, 4, n - 1)),
+            pltpu.SemaphoreType.DMA((cands + 2, 4, n - 1)),
+            pltpu.SemaphoreType.DMA((2, dp - 1)),
         ],
         compiler_params=pltpu.CompilerParams(
             vmem_limit_bytes=56 << 20, collective_id=0, has_side_effects=True
@@ -403,22 +420,8 @@
         name="gradient_features",
     )(hidden_in, query_act, key_act, value_act, ctx_grad, segment_ids,
       down_query, up_query, down_value, up_value,
-      block_rows, tile_rows, block_value[None], tile_value[None], tile_bank)
-    outs = seeds_all.shape[0] // n
-    return pl.pallas_call(
-        functools.partial(tail_kernel, n),
-        out_shape=jax.ShapeDtypeStruct((cands, outs), F32),
-        in_specs=[VMEM] * 2,
-        out_specs=VMEM,
-        scratch_shapes=[
-            pltpu.VMEM((n - 1, cands, KB // n, PB), F32),
-            pltpu.VMEM((n, cands, 2 * outs), F32),
-            pltpu.VMEM((n - 1, cands, 2 * outs), F32),
-            pltpu.SemaphoreType.DMA((4, n - 1)),
-        ],
-        compiler_params=pltpu.CompilerParams(collective_id=1, has_side_effects=True),
-        name="seed_scores",
-    )(feats, seeds_all)
+      block_rows, tile_rows, block_value[None], tile_value[None], tile_bank, seed_feats)
+    return both[:, :outs] * lax.rsqrt(both[:, outs:] / K + EPS) * K ** (-0.5)
 
 
 def solution(mesh):

time: 76.4 us -> 59.2 us (0.77)
  between operations: 13.4 us -> 0.01 us
  Pallas kernels: 60.8 us -> 57.6 us
  other arithmetic: 0 us -> 1.4 us
  local copies, waits for them, and re-layouts: 1.23 us -> 0 us
    pallas_call x2 -> x1, Pallas kernels: 60.8 us -> 57.6 us  [local(): pl.pallas_call(functools.partial(main_kernel, n, dp, kv_count, repeats),...]
    mul x0 -> x1, other arithmetic: none -> 1.4 us  [local(): return both[:, :outs] * lax.rsqrt(both[:, outs:] / K + EPS) * K ** (-0.5)]
    unnamed x1 -> x0, local copies, waits for them, and re-layouts: 1.23 us -> none
  transfers between devices with their start and end apart: 1 -> 0, of which waited for: 0 -> 0; matrix products, arithmetic and copies ran while one was open for 0% -> 0% of each run, Pallas kernels for 66% -> 0%
where the time goes in v3:
time: 59.2 us; the launch traced here: 59 us
  Pallas kernels  57.6 us (97%)
  other arithmetic  1.4 us (2%)
    pallas_call x1, Pallas kernels, local(): pl.pallas_call(functools.partial(main_kernel, n, dp, kv_count, repeats),...  57.6 us
    mul x1, other arithmetic, local(): return both[:, :outs] * lax.rsqrt(both[:, outs:] / K + EPS) * K ** (-0.5)  1.4 us

profile of v3, /device:TPU:0, one launch (start us, length us, event | category | flops | bytes accessed | tf_op | source)
XLA Modules:
  0.0 59.0 jit_solution(16464725669268682518)
XLA Ops:
  0.0 57.6 %gradient_features.1 = f32[2,128]{1,0:T(2,128)} custom-call(bf16[2,512,2048]{2,1,0:T(8,128)(2,1)} %hid.1, bf16[2,512,2048]{2,1,0:T(8,128)(2,1)} %que.1, bf16[2,512,1024]{2,1,0:T(8,128)(2,1)} %key.1, bf16[2,512,1024]{2,1,0:T(8,128)(2,1)} %val.1, bf16[2,512,2048]{2,1,0:T(8,128)(2,1)} %ctx.1, s32[2,512]{1,0:T(2,128)} %seg.1, bf16[2048,128]{1,0:T(8,128)(2,1)} %downq.1, ...), custom_call_target="tpu_custom_call" | custom-call | flops 12884901888 | bytes 16777216 | tf_op jit(solution)/shard_map/gradient_features/pallas_call | solution.py:379
  57.6 1.4 %multiply_multiply_fusion = f32[2,64]{1,0:T(2,128)} fusion(f32[2,128]{1,0:T(2,128)} %gradient_features.1), kind=kLoop, calls=%fused_computation | loop fusion | flops 512 | bytes 1536 | tf_op jit(solution)/shard_map/mul | solution.py:424

commit v4 on v3

--- a/solution.py
+++ b/solution.py
@@ -83,8 +83,9 @@
                 prob_grad = prob_grads[rows, lanes]
                 top = jnp.max(logit, axis=0, keepdims=True)
                 terms = jnp.exp2((logit - top) * (scale * math.log2(math.e)))
-                prob = terms * (1.0 / jnp.sum(terms, axis=0, keepdims=True))
-                delta = jnp.sum(prob * prob_grad, axis=0, keepdims=True)
+                inv = 1.0 / jnp.sum(terms, axis=0, keepdims=True)
+                delta = jnp.sum(terms * prob_grad, axis=0, keepdims=True) * inv
+                prob = terms * inv
 
                 def padded(block):
                     above = jnp.zeros((low - first, DH), BF)
@@ -305,7 +306,7 @@
     out[...] = both
 
 
-CHUNK = 256
+CHUNK = 512
 
 
 def bucket_add(sums, ids, grads, transposed):

time: 59.2 us -> 57.5 us (0.971)
  Pallas kernels: 57.6 us -> 55.9 us
    pallas_call x1, Pallas kernels: 57.6 us -> 55.9 us  [local(): pl.pallas_call(functools.partial(main_kernel, n, dp, kv_count, repeats),...]
where the time goes in v4:
time: 57.5 us; the launch traced here: 57.4 us
  Pallas kernels  55.9 us (97%)
  other arithmetic  1.4 us (2%)
    pallas_call x1, Pallas kernels, local(): pl.pallas_call(functools.partial(main_kernel, n, dp, kv_count, repeats),...  55.9 us
    mul x1, other arithmetic, local(): return both[:, :outs] * lax.rsqrt(both[:, outs:] / K + EPS) * K ** (-0.5)  1.4 us

profile of v4, /device:TPU:0, one launch (start us, length us, event | category | flops | bytes accessed | tf_op | source)
XLA Modules:
  0.0 57.4 jit_solution(5336207058516588645)
XLA Ops:
  0.0 55.9 %gradient_features.1 = f32[2,128]{1,0:T(2,128)} custom-call(bf16[2,512,2048]{2,1,0:T(8,128)(2,1)} %hid.1, bf16[2,512,2048]{2,1,0:T(8,128)(2,1)} %que.1, bf16[2,512,1024]{2,1,0:T(8,128)(2,1)} %key.1, bf16[2,512,1024]{2,1,0:T(8,128)(2,1)} %val.1, bf16[2,512,2048]{2,1,0:T(8,128)(2,1)} %ctx.1, s32[2,512]{1,0:T(2,128)} %seg.1, bf16[2048,128]{1,0:T(8,128)(2,1)} %downq.1, ...), custom_call_target="tpu_custom_call" | custom-call | flops 12884901888 | bytes 16777216 | tf_op jit(solution)/shard_map/gradient_features/pallas_call | solution.py:380
  56.0 1.4 %multiply_multiply_fusion = f32[2,64]{1,0:T(2,128)} fusion(f32[2,128]{1,0:T(2,128)} %gradient_features.1), kind=kLoop, calls=%fused_computation | loop fusion | flops 512 | bytes 1536 | tf_op jit(solution)/shard_map/mul | solution.py:425
